TPU v7x, 512 devices: a whole 4x4x16 slice. The times are simulated.
512 devices in a mesh: ctx: 16 (over y_lo, x, core), mp: 32 (over z, y_hi).
Axes of the slice: x: 4, y: 4 (y_hi: 2, y_lo: 2; y = y_hi * 2 + y_lo), z: 16, core: 2. Of those that a mesh axis runs over, the one named last changes fastest.
Arguments:
- queries: bfloat16 [16384, 4096], P('ctx', 'mp'), may hold values from -320 to 320
- keys_values: bfloat16 [16384, 2048], P('ctx', 'mp'), may hold values from -40 to 40
- query_taps: float32 [4, 4096], P(None, 'mp'), may hold values from -2.5 to 2.5
- pair_taps: float32 [4, 2048], P(None, 'mp'), may hold values from -2.5 to 2.5
- out_gain: float32 [4096], P('mp'), may hold values from 0.1 to 1.9
Outputs:
- head_outputs: bfloat16 [16384, 4096], P('ctx', 'mp')
All inputs are finite; a program needn't handle non-finite values.
Results may differ from a plain program's by a relative error of at most 0.012.
The roundings to bfloat16 on the way count: a program that leaves them out, or rounds other values in their place, can miss the bound.
Values may be sent and summed in bfloat16 or wider, within the bound.
No kernel may reach another device: no remote copies, remote signals or barrier semaphores. Data moves between devices by JAX's collectives and lax.ppermute only.
A program may use at most 64 MiB of HBM per device.

v0:
```python
import math
import jax
import jax.numpy as jnp
from jax import lax
from jax.sharding import PartitionSpec as P

HEAD_CHANNELS = 128
TAPS = 4
TRANSFORM_BLOCK = 128
KEEP = 16
NEGATIVE = -1e30
EPSILON = 1e-06


def shifted(value, axis, steps):
    count = lax.axis_size(axis)
    leading, last = (max(0, -steps), min(count, count - steps))
    return lax.ppermute(value, axis, [(source, source + steps) for source in range(leading, last)])


def from_partner(block, axis, apart):
    count = lax.axis_size(axis)
    route = []
    for low in range(count):
        high = low | 1 << apart
        if high != low and high < count:
            route += [(low, high), (high, low)]
    return lax.ppermute(block, axis, route)


def dct_table():
    frequency = jnp.arange(KEEP, dtype=jnp.float32)[:, None]
    offset = jnp.arange(TRANSFORM_BLOCK, dtype=jnp.float32)[None, :]
    table = jnp.cos(math.pi * (offset + 0.5) * frequency / TRANSFORM_BLOCK) * math.sqrt(
        2.0 / TRANSFORM_BLOCK
    )
    table = jnp.where(frequency == 0.0, table * math.sqrt(0.5), table)
    return table.astype(jnp.bfloat16)


def compress(values):
    blocks = values.reshape(values.shape[0] // TRANSFORM_BLOCK, TRANSFORM_BLOCK, values.shape[1])
    packed = jnp.einsum("jt,btc->bjc", dct_table(), blocks, preferred_element_type=jnp.float32)
    return packed.astype(jnp.bfloat16).reshape(-1, values.shape[1])


def causal_conv(history, values, weights):
    lead = weights.shape[0] - 1
    padded = jnp.concatenate([history, values], 0)
    length = values.shape[0]
    total = weights[0] * values.astype(jnp.float32)
    for shift in range(1, weights.shape[0]):
        total = total + weights[shift] * padded[lead - shift : lead - shift + length].astype(
            jnp.float32
        )
    return total.astype(jnp.bfloat16)


def local_state(query_heads, pairs, score_scale):
    entry_count = query_heads.shape[0] // TRANSFORM_BLOCK
    heads = query_heads.shape[1]
    scores = (
        jnp.einsum(
            "uxwi,umi->uxwm",
            query_heads.reshape(entry_count, TRANSFORM_BLOCK, heads, HEAD_CHANNELS),
            pairs[:, :HEAD_CHANNELS].reshape(entry_count, TRANSFORM_BLOCK, HEAD_CHANNELS),
            preferred_element_type=jnp.float32,
        )
        * score_scale
    )
    causal = (
        jnp.arange(TRANSFORM_BLOCK)[:, None, None] >= jnp.arange(TRANSFORM_BLOCK)[None, None, :]
    )
    scores = jnp.where(causal, scores, NEGATIVE)
    top = jnp.max(scores, -1)
    weights = jnp.where(causal, jnp.exp(scores - top[..., None]), 0.0)
    total = jnp.sum(weights, -1)
    summed = jnp.einsum(
        "cevo,coa->ceva",
        weights.astype(jnp.bfloat16),
        pairs[:, HEAD_CHANNELS:].reshape(entry_count, TRANSFORM_BLOCK, HEAD_CHANNELS),
        preferred_element_type=jnp.float32,
    )
    rows = entry_count * TRANSFORM_BLOCK
    return (
        top.reshape(rows, heads),
        total.reshape(rows, heads),
        summed.reshape(rows, heads, HEAD_CHANNELS),
    )


def attend(state, query_heads, query_blocks, keys, key_blocks, score_scale):
    top, total, summed = state
    entry_count = query_heads.shape[0]
    size = 512
    tops, totals, sums = ([], [], [])
    for begin in range(0, entry_count, size):
        part = query_heads[begin : begin + size]
        scores = (
            jnp.einsum(
                "qhd,kd->qhk", part, keys[:, :HEAD_CHANNELS], preferred_element_type=jnp.float32
            )
            * score_scale
        )
        seen = key_blocks[None, None, :] < query_blocks[begin : begin + size, None, None]
        scores = jnp.where(seen, scores, NEGATIVE)
        old_top = top[begin : begin + size]
        new_top = jnp.maximum(old_top, jnp.max(scores, -1))
        weights = jnp.where(seen, jnp.exp(scores - new_top[..., None]), 0.0)
        rescale = jnp.exp(old_top - new_top)
        totals.append(rescale * total[begin : begin + size] + jnp.sum(weights, -1))
        sums.append(
            rescale[..., None] * summed[begin : begin + size]
            + jnp.einsum(
                "qhk,kd->qhd",
                weights.astype(jnp.bfloat16),
                keys[:, HEAD_CHANNELS:],
                preferred_element_type=jnp.float32,
            )
        )
        tops.append(new_top)
    return (jnp.concatenate(tops, 0), jnp.concatenate(totals, 0), jnp.concatenate(sums, 0))


def per_device(queries, keys_values, query_taps, pair_taps, out_gain):
    rows = queries.shape[0]
    span_rows = rows // 2
    per_span = span_rows // TRANSFORM_BLOCK
    shards = lax.axis_size("ctx")
    place = lax.axis_index("ctx")
    member = lax.axis_index("mp")
    score_scale = 1.0 / math.sqrt(HEAD_CHANNELS)
    tail = TAPS - 1
    columns = queries.shape[1]
    first_tail = jnp.concatenate(
        [queries[span_rows - tail : span_rows], keys_values[span_rows - tail : span_rows]], 1
    )
    second_tail = jnp.concatenate([queries[rows - tail :], keys_values[rows - tail :]], 1)
    from_lower = shifted(first_tail, "ctx", 1)
    from_upper = shifted(second_tail, "ctx", -1)
    before_second = jnp.where(place == shards - 1, first_tail, from_upper)
    query_conv = jnp.concatenate(
        [
            causal_conv(from_lower[:, :columns], queries[:span_rows], query_taps),
            causal_conv(before_second[:, :columns], queries[span_rows:], query_taps),
        ],
        0,
    )
    pair_conv = jnp.concatenate(
        [
            causal_conv(from_lower[:, columns:], keys_values[:span_rows], pair_taps),
            causal_conv(before_second[:, columns:], keys_values[span_rows:], pair_taps),
        ],
        0,
    )
    width = keys_values.shape[1]
    rounds = (2 * HEAD_CHANNELS // width).bit_length() - 1

    def join(mine, other, bit):
        lower = member // 2**bit % 2 == 0
        return jnp.where(
            lower, jnp.concatenate([mine, other], 1), jnp.concatenate([other, mine], 1)
        )

    pairs = pair_conv
    packed = compress(pair_conv)
    for bit in range(rounds):
        other = from_partner(jnp.concatenate([pairs, packed], 0), "mp", bit)
        pairs = join(pairs, other[:rows], bit)
        packed = join(packed, other[rows:], bit)
    heads_here = columns // HEAD_CHANNELS
    query_heads = query_conv.reshape(rows, heads_here, HEAD_CHANNELS)
    own_rows = jnp.arange(rows)
    own_span = jnp.where(own_rows < span_rows, place, 2 * shards - 1 - place)
    query_blocks = own_span * per_span + own_rows % span_rows // TRANSFORM_BLOCK
    state = local_state(query_heads, pairs, score_scale)
    shard_rows = rows * KEEP // TRANSFORM_BLOCK
    half_rows = shard_rows // 2
    piece = lax.all_gather(packed, "ctx", axis=0, tiled=True)
    positions = jnp.arange(piece.shape[0])
    owner = positions // shard_rows
    within = positions % shard_rows
    span_index = jnp.where(within < half_rows, owner, 2 * shards - 1 - owner)
    key_blocks = span_index * per_span + within % half_rows // KEEP
    state = attend(state, query_heads, query_blocks, piece, key_blocks, score_scale)
    top, total, summed = state
    attended = summed / total[..., None]
    normed = attended * lax.rsqrt(jnp.mean(attended * attended, -1, keepdims=True) + EPSILON)
    return (normed.reshape(rows, columns) * out_gain).astype(jnp.bfloat16)


def solution(mesh):
    in_specs = (P("ctx", "mp"), P("ctx", "mp"), P(None, "mp"), P(None, "mp"), P("mp"))
    out_specs = P("ctx", "mp")
    return jax.shard_map(
        per_device, mesh=mesh, in_specs=in_specs, out_specs=out_specs, check_vma=False
    )
```

profile of v0, /device:TPU:1, one launch (start us, length us, event | category | flops | bytes accessed | tf_op | source)
XLA Modules:
  0.0 103.2 jit_solution(5550732140074275808)
XLA Ops:
  6.5 0.7 fusion.93
  7.2 0.8 fusion.95
  8.2 8.8 %collective-permute-start.1 = (bf16[3,192]{1,0:T(4,128)(2,1)S(1)}, bf16[3,192]{1,0:T(4,128)(2,1)S(1)}, u32[]{:S(2)}, u32[]{:S(2)}) collective-permute-start(bf16[3,192]{1,0:T(4,128)(2,1)S(1)} %pad_maximum_fusion.9), channel_id=1, source_target_pairs={{32,0},{64,32},{96,64},{128,96},{160,128},{192,160},{224,192},{256... | collective-permute-start | bytes 3464 | tf_op jit(solution)/shard_map/ppermute | solution.py:18
  17.0 0.9 fusion.94
  17.8 0.8 slice_bitcast_fusion.3
  18.8 1.9 %collective-permute-start = (bf16[3,192]{1,0:T(4,128)(2,1)S(1)}, bf16[3,192]{1,0:T(4,128)(2,1)S(1)}, u32[]{:S(2)}, u32[]{:S(2)}) collective-permute-start(bf16[3,192]{1,0:T(4,128)(2,1)S(1)} %get-tuple-element.37), channel_id=1, source_target_pairs={{0,32},{32,64},{64,96},{96,128},{128,160},{160,192},{192,224},{224... | collective-permute-start | bytes 3464 | tf_op jit(solution)/shard_map/ppermute | solution.py:18
  20.9 1.0 collective-permute-done
  22.6 1.9 %collective-permute-start.2 = (bf16[1152,64]{0,1:T(8,128)(2,1)S(1)}, bf16[1152,64]{0,1:T(8,128)(2,1)S(1)}, u32[]{:S(2)}, u32[]{:S(2)}) collective-permute-start(bf16[1152,64]{0,1:T(8,128)(2,1)S(1)} %pad_maximum_fusion.2), channel_id=1, source_target_pairs={{0,1},{1,0},{2,3},{3,2},{4,5},{5,4},{6,7},{7,6},{8,9},{9,8},{10,11... | collective-permute-start | bytes 442376 | tf_op jit(solution)/shard_map/ppermute | solution.py:28
  24.5 0.8 slice_bitcast_fusion.7
  25.4 5.9 %collective-permute-done.2 = bf16[1152,64]{0,1:T(8,128)(2,1)S(1)} collective-permute-done((bf16[1152,64]{0,1:T(8,128)(2,1)S(1)}, bf16[1152,64]{0,1:T(8,128)(2,1)S(1)}, u32[]{:S(2)}, u32[]{:S(2)}) %collective-permute-start.2) | collective-permute-done | bytes 147488 | tf_op jit(solution)/shard_map/ppermute | solution.py:28
  31.4 1.9 %collective-permute-start.3 = (bf16[1152,128]{0,1:T(8,128)(2,1)S(1)}, bf16[1152,128]{0,1:T(8,128)(2,1)S(1)}, u32[]{:S(2)}, u32[]{:S(2)}) collective-permute-start(bf16[1152,128]{0,1:T(8,128)(2,1)S(1)} %pad_maximum_fusion), channel_id=1, source_target_pairs={{0,2},{2,0},{1,3},{3,1},{4,6},{6,4},{5,7},{7,5},{8,10},{10,8},{9,1... | collective-permute-start | bytes 884744 | tf_op jit(solution)/shard_map/ppermute | solution.py:28
  33.4 1.0 fusion.92
  34.4 6.5 %collective-permute-done.3 = bf16[1152,128]{0,1:T(8,128)(2,1)S(1)} collective-permute-done((bf16[1152,128]{0,1:T(8,128)(2,1)S(1)}, bf16[1152,128]{0,1:T(8,128)(2,1)S(1)}, u32[]{:S(2)}, u32[]{:S(2)}) %collective-permute-start.3) | collective-permute-done | bytes 294944 | tf_op jit(solution)/shard_map/ppermute | solution.py:28
  40.9 0.6 maximum_select_fusion.2
  42.4 0.3 fusion.99
  42.9 0.3 fusion.30
  43.2 43.6 %all-gather.2.cloned.1.call-done = bf16[2048,256]{0,1:T(8,128)(2,1)} async-done(((bf16[128,256]{0,1:T(8,128)(2,1)}), bf16[2048,256]{0,1:T(8,128)(2,1)}) %all-gather.2.cloned.1.call-update) | async-done | bytes 1048592 | tf_op jit(solution)/shard_map/all_gather | solution.py:179
  86.8 2.0 %fusion = (f32[512]{0:T(512)S(1)}, f32[512,2048]{1,0:T(8,128)S(1)}) fusion(s32[2048]{0:T(1024)S(1)} %fusion.52, s32[512]{0:T(512)S(1)} %get-tuple-element.28, bf16[512,128]{1,0:T(8,128)(2,1)S(1)} %get-tuple-element.29, bf16[2048,256]{0,1:T(8,128)(2,1)} %all-gather.2.cloned.1.call-done), kind=kOutput, calls=%fused_computation.4 | convolution fusion | flops 272629248 | bytes 4861952 | tf_op jit(solution)/shard_map/qhd,kd->qhk/dot_general | solution.py:100
  88.9 2.1 %fusion.2 = (f32[512]{0:T(512)S(1)}, f32[512]{0:T(512)S(1)}, f32[512,2048]{1,0:T(8,128)S(1)}) fusion(f32[512,2048]{1,0:T(8,128)S(1)} %get-tuple-element.46, f32[512]{0:T(512)S(1)} %get-tuple-element.20, s32[2048]{0:T(1024)S(1)} %fusion.52, s32[512]{0:T(512)S(1)} %get-tuple-element.28, s32[512]{0:T(512)S(1)} %get-tuple-element.27, ...), kind=kOutput, calls=%fused_computation.6 | convolution fusion | flops 278920192 | bytes 9062400 | tf_op jit(solution)/shard_map/qhd,kd->qhk/dot_general | solution.py:100
  91.0 1.3 %fusion.4 = f32[512]{0:T(512)S(1)} fusion(f32[512,2048]{1,0:T(8,128)S(1)} %get-tuple-element.47, f32[512]{0:T(512)S(1)} %get-tuple-element.21, s32[2048]{0:T(1024)S(1)} %fusion.52, s32[512]{0:T(512)S(1)} %get-tuple-element.27), kind=kLoop, calls=%fused_computation.8 | loop fusion | flops 6290944 | bytes 4208640 | tf_op jit(solution)/shard_map/reduce_sum | solution.py:111
  92.5 1.2 %fusion.11 = f32[512,128]{1,0:T(8,128)S(1)} fusion(f32[512,128]{1,0:T(8,128)S(1)} %get-tuple-element.49, f32[512,2048]{1,0:T(8,128)S(1)} %get-tuple-element.46, f32[512]{0:T(512)S(1)} %get-tuple-element.20, s32[2048]{0:T(1024)S(1)} %fusion.52, s32[512]{0:T(512)S(1)} %get-tuple-element.28, bf16[2048,256]{0,1:T(8,128)(2,1)S(1)} %copy-done.1), kind=kOutput, calls=%fused_computation.14 | convolution fusion | flops 274792448 | bytes 5255168 | tf_op jit(solution)/shard_map/qhk,kd->qhd/dot_general | solution.py:114
  93.7 1.2 %fusion.14 = f32[512,128]{1,0:T(8,128)S(1)} fusion(f32[512,128]{1,0:T(8,128)S(1)} %get-tuple-element.48, f32[512,2048]{1,0:T(8,128)S(1)} %get-tuple-element.47, f32[512]{0:T(512)S(1)} %get-tuple-element.21, s32[2048]{0:T(1024)S(1)} %fusion.52, s32[512]{0:T(512)S(1)} %get-tuple-element.27, bf16[2048,256]{0,1:T(8,128)(2,1)S(1)} %copy-done.1), kind=kOutput, calls=%fused_computation.15 | convolution fusion | flops 274792448 | bytes 5255168 | tf_op jit(solution)/shard_map/qhk,kd->qhd/dot_general | solution.py:114
  94.9 0.4 fusion.21
  95.3 1.0 %fusion.20 = bf16[1024,128]{1,0:T(8,128)(2,1)} fusion(f32[512,128]{1,0:T(8,128)S(1)} %fusion.14, f32[512,128]{1,0:T(8,128)S(1)} %fusion.11, f32[128]{0:T(128)S(1)} %copy-done, f32[1024]{0:T(1024)S(1)} %add_rsqrt_fusion, f32[1024]{0:T(1024)S(1)} %bitcast.72), kind=kLoop, calls=%fused_computation.24 | loop fusion | flops 655360 | bytes 795136 | tf_op jit(solution)/shard_map/convert_element_type | solution.py:189
  (50 shorter events, 2.4 us)
Async XLA Ops:
  6.5 80.2 %all-gather.2.cloned.1.call-start = ((), (), s32[]{:S(2)}) async-start(), calls=%async_computation | async-start | bytes 1114112 | tf_op jit(solution)/shard_map/all_gather | solution.py:179
  8.2 10.7 %collective-permute-start.1 = (bf16[3,192]{1,0:T(4,128)(2,1)S(1)}, bf16[3,192]{1,0:T(4,128)(2,1)S(1)}, u32[]{:S(2)}, u32[]{:S(2)}) collective-permute-start(bf16[3,192]{1,0:T(4,128)(2,1)S(1)} %pad_maximum_fusion.9), channel_id=1, source_target_pairs={{32,0},{64,32},{96,64},{128,96},{160,128},{192,160},{224,192},{256... | collective-permute-start | bytes 3464 | tf_op jit(solution)/shard_map/ppermute | solution.py:18
  18.8 3.1 %collective-permute-start = (bf16[3,192]{1,0:T(4,128)(2,1)S(1)}, bf16[3,192]{1,0:T(4,128)(2,1)S(1)}, u32[]{:S(2)}, u32[]{:S(2)}) collective-permute-start(bf16[3,192]{1,0:T(4,128)(2,1)S(1)} %get-tuple-element.37), channel_id=1, source_target_pairs={{0,32},{32,64},{64,96},{96,128},{128,160},{160,192},{192,224},{224... | collective-permute-start | bytes 3464 | tf_op jit(solution)/shard_map/ppermute | solution.py:18
  22.6 8.7 %collective-permute-start.2 = (bf16[1152,64]{0,1:T(8,128)(2,1)S(1)}, bf16[1152,64]{0,1:T(8,128)(2,1)S(1)}, u32[]{:S(2)}, u32[]{:S(2)}) collective-permute-start(bf16[1152,64]{0,1:T(8,128)(2,1)S(1)} %pad_maximum_fusion.2), channel_id=1, source_target_pairs={{0,1},{1,0},{2,3},{3,2},{4,5},{5,4},{6,7},{7,6},{8,9},{9,8},{10,11... | collective-permute-start | bytes 442376 | tf_op jit(solution)/shard_map/ppermute | solution.py:28
  31.4 9.4 %collective-permute-start.3 = (bf16[1152,128]{0,1:T(8,128)(2,1)S(1)}, bf16[1152,128]{0,1:T(8,128)(2,1)S(1)}, u32[]{:S(2)}, u32[]{:S(2)}) collective-permute-start(bf16[1152,128]{0,1:T(8,128)(2,1)S(1)} %pad_maximum_fusion), channel_id=1, source_target_pairs={{0,2},{2,0},{1,3},{3,1},{4,6},{6,4},{5,7},{7,5},{8,10},{10,8},{9,1... | collective-permute-start | bytes 884744 | tf_op jit(solution)/shard_map/ppermute | solution.py:28
  86.8 2.1 %copy-start.1 = (bf16[2048,256]{0,1:T(8,128)(2,1)S(1)}, bf16[2048,256]{0,1:T(8,128)(2,1)}, u32[]{:S(2)}) copy-start(bf16[2048,256]{0,1:T(8,128)(2,1)} %all-gather.2.cloned.1.call-done) | copy-start | bytes 3145732
  93.7 1.6 %copy-start = (f32[128]{0:T(128)S(1)}, f32[128]{0:T(128)}, u32[]{:S(2)}) copy-start(f32[128]{0:T(128)} %param.9) | copy-start | bytes 1540
Sparse Core Ops, SparseCore 0:
  41.7 45.0 all-gather.1
where the time goes:
time: 104 us; the launch traced here: 103 us
  waiting for transfers between devices  57 us (55%)
  starting transfers between devices  14.6 us (14%)
  between operations  13.7 us (13%)
  matrix products  7.34 us (7%)
  local copies, waits for them, and re-layouts  6.06 us (6%)
  other arithmetic  4.51 us (4%)
    all_gather x1, waiting for transfers between devices, per_device(): piece = lax.all_gather(packed, 'ctx', axis=0, tiled=True)  43.6 us
    ppermute x2, waiting for transfers between devices, from_partner(): return lax.ppermute(block, axis, route)  12.4 us
    ppermute x2, starting transfers between devices, shifted(): lax.ppermute(value, axis, [(source, source + steps) for source in range(l...  10.7 us
    dot_general x2, matrix products, attend(): jnp.einsum('qhd,kd->qhk', part, keys[:, :HEAD_CHANNELS], preferred_elemen...  4.17 us
    ppermute x2, starting transfers between devices, from_partner(): return lax.ppermute(block, axis, route)  3.84 us
    dot_general x2, matrix products, attend(): jnp.einsum('qhk,kd->qhd', weights.astype(jnp.bfloat16), keys[:, HEAD_CHAN...  2.36 us
  transfers between devices with their start and end apart: 5, of which 4 were waited for; matrix products, arithmetic and copies ran while one was open for 5% of the time, Pallas kernels for 0%

commit v1 on v0

--- a/solution.py
+++ b/solution.py
@@ -3,6 +3,7 @@
 import jax.numpy as jnp
 from jax import lax
 from jax.sharding import PartitionSpec as P
+from jax.lax import all_to_all, axis_size
 
 HEAD_CHANNELS = 128
 TAPS = 4
@@ -176,7 +177,15 @@
     state = local_state(query_heads, pairs, score_scale)
     shard_rows = rows * KEEP // TRANSFORM_BLOCK
     half_rows = shard_rows // 2
-    piece = lax.all_gather(packed, "ctx", axis=0, tiled=True)
+    piece = jnp.concatenate(
+        all_to_all(
+            jnp.stack([packed for _ in range(axis_size("ctx"))], 0),
+            "ctx",
+            split_axis=0,
+            concat_axis=0,
+        ),
+        0,
+    )
     positions = jnp.arange(piece.shape[0])
     owner = positions // shard_rows
     within = positions % shard_rows

time: 104 us -> 67.8 us (0.65)
  waiting for transfers between devices: 57 us -> 29.8 us
  between operations: 13.7 us -> 0.39 us
  starting transfers between devices: 14.6 us -> 19.9 us
  matrix products: 7.34 us -> 6.14 us
  local copies, waits for them, and re-layouts: 6.06 us -> 7.23 us
    all_gather x1 -> x0, waiting for transfers between devices: 43.6 us -> none  [per_device(): piece = lax.all_gather(packed, 'ctx', axis=0, tiled=True)]
    all_to_all x0 -> x1, waiting for transfers between devices: none -> 15 us  [per_device(): all_to_all(jnp.stack([packed for _ in range(axis_size('ctx'))], 0), 'ctx'...]
    all_to_all x0 -> x1, starting transfers between devices: none -> 5.33 us  [per_device(): all_to_all(jnp.stack([packed for _ in range(axis_size('ctx'))], 0), 'ctx'...]
    ppermute x2, waiting for transfers between devices: 12.4 us -> 13.9 us  [from_partner(): return lax.ppermute(block, axis, route)]
    dot_general x2, matrix products: 4.17 us -> 3.01 us  [attend(): jnp.einsum('qhd,kd->qhk', part, keys[:, :HEAD_CHANNELS], preferred_elemen...]
    another operation x0 -> x1, local copies, waits for them, and re-layouts: none -> 1.07 us  [per_device(): jnp.stack([packed for _ in range(axis_size('ctx'))], 0)]
  transfers between devices with their start and end apart: 5 -> 5, of which waited for: 4 -> 4; matrix products, arithmetic and copies ran while one was open for 5% -> 7% of each run, Pallas kernels for 0% -> 0%
where the time goes in v1:
time: 67.8 us; the launch traced here: 67.4 us
  waiting for transfers between devices  29.8 us (44%)
  starting transfers between devices  19.9 us (29%)
  local copies, waits for them, and re-layouts  7.23 us (11%)
  matrix products  6.14 us (9%)
  other arithmetic  3.88 us (6%)
    all_to_all x1, waiting for transfers between devices, per_device(): all_to_all(jnp.stack([packed for _ in range(axis_size('ctx'))], 0), 'ctx'...  15 us
    ppermute x2, waiting for transfers between devices, from_partner(): return lax.ppermute(block, axis, route)  13.9 us
    ppermute x2, starting transfers between devices, shifted(): lax.ppermute(value, axis, [(source, source + steps) for source in range(l...  10.7 us
    all_to_all x1, starting transfers between devices, per_device(): all_to_all(jnp.stack([packed for _ in range(axis_size('ctx'))], 0), 'ctx'...  5.33 us
    ppermute x2, starting transfers between devices, from_partner(): return lax.ppermute(block, axis, route)  3.84 us
    dot_general x2, matrix products, attend(): jnp.einsum('qhd,kd->qhk', part, keys[:, :HEAD_CHANNELS], preferred_elemen...  3.01 us
    dot_general x2, matrix products, attend(): jnp.einsum('qhk,kd->qhd', weights.astype(jnp.bfloat16), keys[:, HEAD_CHAN...  2.34 us
    mul x2, local copies, waits for them, and re-layouts, causal_conv(): total = weights[0] * values.astype(jnp.float32)  1.67 us
  transfers between devices with their start and end apart: 5, of which 4 were waited for; matrix products, arithmetic and copies ran while one was open for 7% of the time, Pallas kernels for 0%

profile of v1, /device:TPU:1, one launch (start us, length us, event | category | flops | bytes accessed | tf_op | source)
XLA Modules:
  0.0 67.4 jit_solution(18118026835854042903)
XLA Ops:
  0.0 0.7 %fusion.93 = (bf16[3,128]{1,0:T(4,128)(2,1)S(1)}, bf16[3,128]{1,0:T(4,128)(2,1)S(1)}) fusion(bf16[1024,128]{1,0:T(8,128)(2,1)} %param.5), kind=kLoop, calls=%fused_computation.168 | loop fusion | bytes 3072 | tf_op jit(solution)/shard_map/slice | solution.py:137
  0.7 0.8 %fusion.95 = (bf16[3,64]{0,1:T(8,128)(2,1)S(1)}, bf16[3,64]{0,1:T(8,128)(2,1)S(1)}) fusion(bf16[1024,64]{0,1:T(8,128)(2,1)} %param.6), kind=kLoop, calls=%fused_computation.170 | loop fusion | bytes 1536 | tf_op jit(solution)/shard_map/slice | solution.py:137
  1.6 8.8 %collective-permute-start.1 = (bf16[3,192]{1,0:T(4,128)(2,1)S(1)}, bf16[3,192]{1,0:T(4,128)(2,1)S(1)}, u32[]{:S(2)}, u32[]{:S(2)}) collective-permute-start(bf16[3,192]{1,0:T(4,128)(2,1)S(1)} %pad_maximum_fusion.9), channel_id=1, source_target_pairs={{32,0},{64,32},{96,64},{128,96},{160,128},{192,160},{224,192},{256... | collective-permute-start | bytes 3464 | tf_op jit(solution)/shard_map/ppermute | solution.py:19
  10.4 0.9 %fusion.94 = (bf16[512,64]{0,1:T(8,128)(2,1)S(1)}, bf16[512,64]{0,1:T(8,128)(2,1)S(1)}) fusion(bf16[1024,64]{0,1:T(8,128)(2,1)} %param.6), kind=kLoop, calls=%fused_computation.169 | loop fusion | bytes 262144 | tf_op jit(solution)/shard_map/slice | solution.py:152
  11.3 1.0 %fusion.92 = (bf16[512,128]{1,0:T(8,128)(2,1)S(1)}, bf16[512,128]{1,0:T(8,128)(2,1)S(1)}) fusion(bf16[1024,128]{1,0:T(8,128)(2,1)} %param.5), kind=kLoop, calls=%fused_computation.167 | loop fusion | bytes 524288 | tf_op jit(solution)/shard_map/slice | solution.py:145
  12.3 0.8 %slice_bitcast_fusion.7 = (f32[128]{0:T(128)S(1)}, f32[128]{0:T(128)S(1)}, f32[128]{0:T(128)S(1)}, f32[128]{0:T(128)S(1)}) fusion(f32[4,128]{1,0:T(4,128)} %param.7), kind=kLoop, calls=%fused_computation.154 | loop fusion | bytes 4096 | tf_op jit(solution)/shard_map/mul | solution.py:52
  13.1 0.8 %slice_bitcast_fusion.3 = (f32[64]{0:T(128)S(1)}, f32[64]{0:T(128)S(1)}, f32[64]{0:T(128)S(1)}, f32[64]{0:T(128)S(1)}) fusion(f32[4,64]{1,0:T(4,128)} %param.8), kind=kLoop, calls=%fused_computation.150 | loop fusion | bytes 2048 | tf_op jit(solution)/shard_map/mul | solution.py:52
  14.1 1.9 %collective-permute-start = (bf16[3,192]{1,0:T(4,128)(2,1)S(1)}, bf16[3,192]{1,0:T(4,128)(2,1)S(1)}, u32[]{:S(2)}, u32[]{:S(2)}) collective-permute-start(bf16[3,192]{1,0:T(4,128)(2,1)S(1)} %get-tuple-element.37), channel_id=1, source_target_pairs={{0,32},{32,64},{64,96},{96,128},{128,160},{160,192},{192,224},{224... | collective-permute-start | bytes 3464 | tf_op jit(solution)/shard_map/ppermute | solution.py:19
  16.2 1.0 %collective-permute-done = bf16[3,192]{1,0:T(4,128)(2,1)S(1)} collective-permute-done((bf16[3,192]{1,0:T(4,128)(2,1)S(1)}, bf16[3,192]{1,0:T(4,128)(2,1)S(1)}, u32[]{:S(2)}, u32[]{:S(2)}) %collective-permute-start) | collective-permute-done | bytes 1184 | tf_op jit(solution)/shard_map/ppermute | solution.py:19
  17.9 1.9 %collective-permute-start.2 = (bf16[1152,64]{0,1:T(8,128)(2,1)S(1)}, bf16[1152,64]{0,1:T(8,128)(2,1)S(1)}, u32[]{:S(2)}, u32[]{:S(2)}) collective-permute-start(bf16[1152,64]{0,1:T(8,128)(2,1)S(1)} %pad_maximum_fusion.2), channel_id=1, source_target_pairs={{0,1},{1,0},{2,3},{3,2},{4,5},{5,4},{6,7},{7,6},{8,9},{9,8},{10,11... | collective-permute-start | bytes 442376 | tf_op jit(solution)/shard_map/ppermute | solution.py:29
  19.9 6.7 %collective-permute-done.2 = bf16[1152,64]{0,1:T(8,128)(2,1)S(1)} collective-permute-done((bf16[1152,64]{0,1:T(8,128)(2,1)S(1)}, bf16[1152,64]{0,1:T(8,128)(2,1)S(1)}, u32[]{:S(2)}, u32[]{:S(2)}) %collective-permute-start.2) | collective-permute-done | bytes 147488 | tf_op jit(solution)/shard_map/ppermute | solution.py:29
  26.7 1.9 %collective-permute-start.3 = (bf16[1152,128]{0,1:T(8,128)(2,1)S(1)}, bf16[1152,128]{0,1:T(8,128)(2,1)S(1)}, u32[]{:S(2)}, u32[]{:S(2)}) collective-permute-start(bf16[1152,128]{0,1:T(8,128)(2,1)S(1)} %pad_maximum_fusion), channel_id=1, source_target_pairs={{0,2},{2,0},{1,3},{3,1},{4,6},{6,4},{5,7},{7,5},{8,10},{10,8},{9,1... | collective-permute-start | bytes 884744 | tf_op jit(solution)/shard_map/ppermute | solution.py:29
  29.0 7.2 %collective-permute-done.3 = bf16[1152,128]{0,1:T(8,128)(2,1)S(1)} collective-permute-done((bf16[1152,128]{0,1:T(8,128)(2,1)S(1)}, bf16[1152,128]{0,1:T(8,128)(2,1)S(1)}, u32[]{:S(2)}, u32[]{:S(2)}) %collective-permute-start.3) | collective-permute-done | bytes 294944 | tf_op jit(solution)/shard_map/ppermute | solution.py:29
  36.7 1.1 %stack.2 = bf16[16,128,256]{2,1,0:T(8,128)(2,1)} broadcast(bf16[128,256]{1,0:T(8,128)(2,1)S(1)} %copy.38), dimensions={1,2} | broadcast | bytes 1114112 | tf_op jit(solution)/shard_map/stack | solution.py:182
  37.8 5.3 %all-to-all-start = ((bf16[16,128,256]{2,1,0:T(8,128)(2,1)}), bf16[16,128,256]{2,1,0:T(8,128)(2,1)S(1)}, u32[]{:S(2)}, u32[]{:S(2)}) async-start(bf16[16,128,256]{2,1,0:T(8,128)(2,1)} %stack.2), calls=%async_computation | async-start | bytes 2097152 | tf_op jit(solution)/shard_map/all_to_all | solution.py:181
  43.1 0.3 fusion.99
  44.1 15.0 %all-to-all-done = bf16[16,128,256]{2,1,0:T(8,128)(2,1)S(1)} async-done(((bf16[16,128,256]{2,1,0:T(8,128)(2,1)}), bf16[16,128,256]{2,1,0:T(8,128)(2,1)S(1)}, u32[]{:S(2)}, u32[]{:S(2)}) %all-to-all-start) | async-done | bytes 1048608 | tf_op jit(solution)/shard_map/all_to_all | solution.py:181
  59.0 0.9 %fusion = (f32[512]{0:T(512)S(1)}, f32[512,2048]{1,0:T(8,128)S(1)}) fusion(s32[2048]{0:T(1024)S(1)} %fusion.52, s32[512]{0:T(512)S(1)} %get-tuple-element.28, bf16[512,128]{1,0:T(8,128)(2,1)S(1)} %get-tuple-element.29, bf16[2048,256]{1,0:T(8,128)(2,1)S(1)} %bitcast.67), kind=kOutput, calls=%fused_computation.4 | convolution fusion | flops 272629248 | bytes 4861952 | tf_op jit(solution)/shard_map/qhd,kd->qhk/dot_general | solution.py:101
  60.0 2.1 %fusion.2 = (f32[512]{0:T(512)S(1)}, f32[512]{0:T(512)S(1)}, f32[512,2048]{1,0:T(8,128)S(1)}) fusion(f32[512,2048]{1,0:T(8,128)S(1)} %get-tuple-element.46, f32[512]{0:T(512)S(1)} %get-tuple-element.20, s32[2048]{0:T(1024)S(1)} %fusion.52, s32[512]{0:T(512)S(1)} %get-tuple-element.28, s32[512]{0:T(512)S(1)} %get-tuple-element.27, ...), kind=kOutput, calls=%fused_computation.6 | convolution fusion | flops 278920192 | bytes 9062400 | tf_op jit(solution)/shard_map/qhd,kd->qhk/dot_general | solution.py:101
  62.3 1.2 %fusion.11 = f32[512,128]{1,0:T(8,128)S(1)} fusion(f32[512,128]{1,0:T(8,128)S(1)} %get-tuple-element.49, f32[512,2048]{1,0:T(8,128)S(1)} %get-tuple-element.46, f32[512]{0:T(512)S(1)} %get-tuple-element.20, s32[2048]{0:T(1024)S(1)} %fusion.52, s32[512]{0:T(512)S(1)} %get-tuple-element.28, bf16[2048,256]{1,0:T(8,128)(2,1)S(1)} %bitcast.69), kind=kOutput, calls=%fused_computation.14 | convolution fusion | flops 274792448 | bytes 5255168 | tf_op jit(solution)/shard_map/qhk,kd->qhd/dot_general | solution.py:115
  63.5 1.2 %fusion.4 = f32[512]{0:T(512)S(1)} fusion(f32[512,2048]{1,0:T(8,128)S(1)} %get-tuple-element.47, f32[512]{0:T(512)S(1)} %get-tuple-element.21, s32[2048]{0:T(1024)S(1)} %fusion.52, s32[512]{0:T(512)S(1)} %get-tuple-element.27), kind=kLoop, calls=%fused_computation.8 | loop fusion | flops 6290944 | bytes 4208640 | tf_op jit(solution)/shard_map/reduce_sum | solution.py:112
  64.7 1.2 %fusion.14 = f32[512,128]{1,0:T(8,128)S(1)} fusion(f32[512,128]{1,0:T(8,128)S(1)} %get-tuple-element.48, f32[512,2048]{1,0:T(8,128)S(1)} %get-tuple-element.47, f32[512]{0:T(512)S(1)} %get-tuple-element.21, s32[2048]{0:T(1024)S(1)} %fusion.52, s32[512]{0:T(512)S(1)} %get-tuple-element.27, bf16[2048,256]{1,0:T(8,128)(2,1)S(1)} %bitcast.70), kind=kOutput, calls=%fused_computation.15 | convolution fusion | flops 274792448 | bytes 5255168 | tf_op jit(solution)/shard_map/qhk,kd->qhd/dot_general | solution.py:115
  65.9 0.4 fusion.21
  66.3 1.0 %fusion.20 = bf16[1024,128]{1,0:T(8,128)(2,1)} fusion(f32[512,128]{1,0:T(8,128)S(1)} %fusion.14, f32[512,128]{1,0:T(8,128)S(1)} %fusion.11, f32[128]{0:T(128)S(1)} %copy-done, f32[1024]{0:T(1024)S(1)} %add_rsqrt_fusion, f32[1024]{0:T(1024)S(1)} %bitcast.77), kind=kLoop, calls=%fused_computation.24 | loop fusion | flops 655360 | bytes 795136 | tf_op jit(solution)/shard_map/convert_element_type | solution.py:198
  (49 shorter events, 2.8 us)
Async XLA Ops:
  1.6 12.5 %collective-permute-start.1 = (bf16[3,192]{1,0:T(4,128)(2,1)S(1)}, bf16[3,192]{1,0:T(4,128)(2,1)S(1)}, u32[]{:S(2)}, u32[]{:S(2)}) collective-permute-start(bf16[3,192]{1,0:T(4,128)(2,1)S(1)} %pad_maximum_fusion.9), channel_id=1, source_target_pairs={{32,0},{64,32},{96,64},{128,96},{160,128},{192,160},{224,192},{256... | collective-permute-start | bytes 3464 | tf_op jit(solution)/shard_map/ppermute | solution.py:19
  14.1 3.1 %collective-permute-start = (bf16[3,192]{1,0:T(4,128)(2,1)S(1)}, bf16[3,192]{1,0:T(4,128)(2,1)S(1)}, u32[]{:S(2)}, u32[]{:S(2)}) collective-permute-start(bf16[3,192]{1,0:T(4,128)(2,1)S(1)} %get-tuple-element.37), channel_id=1, source_target_pairs={{0,32},{32,64},{64,96},{96,128},{128,160},{160,192},{192,224},{224... | collective-permute-start | bytes 3464 | tf_op jit(solution)/shard_map/ppermute | solution.py:19
  17.9 8.7 %collective-permute-start.2 = (bf16[1152,64]{0,1:T(8,128)(2,1)S(1)}, bf16[1152,64]{0,1:T(8,128)(2,1)S(1)}, u32[]{:S(2)}, u32[]{:S(2)}) collective-permute-start(bf16[1152,64]{0,1:T(8,128)(2,1)S(1)} %pad_maximum_fusion.2), channel_id=1, source_target_pairs={{0,1},{1,0},{2,3},{3,2},{4,5},{5,4},{6,7},{7,6},{8,9},{9,8},{10,11... | collective-permute-start | bytes 442376 | tf_op jit(solution)/shard_map/ppermute | solution.py:29
  26.7 9.4 %collective-permute-start.3 = (bf16[1152,128]{0,1:T(8,128)(2,1)S(1)}, bf16[1152,128]{0,1:T(8,128)(2,1)S(1)}, u32[]{:S(2)}, u32[]{:S(2)}) collective-permute-start(bf16[1152,128]{0,1:T(8,128)(2,1)S(1)} %pad_maximum_fusion), channel_id=1, source_target_pairs={{0,2},{2,0},{1,3},{3,1},{4,6},{6,4},{5,7},{7,5},{8,10},{10,8},{9,1... | collective-permute-start | bytes 884744 | tf_op jit(solution)/shard_map/ppermute | solution.py:29
  37.8 21.3 %all-to-all-start = ((bf16[16,128,256]{2,1,0:T(8,128)(2,1)}), bf16[16,128,256]{2,1,0:T(8,128)(2,1)S(1)}, u32[]{:S(2)}, u32[]{:S(2)}) async-start(bf16[16,128,256]{2,1,0:T(8,128)(2,1)} %stack.2), calls=%async_computation | async-start | bytes 2097152 | tf_op jit(solution)/shard_map/all_to_all | solution.py:181
  64.7 1.6 %copy-start = (f32[128]{0:T(128)S(1)}, f32[128]{0:T(128)}, u32[]{:S(2)}) copy-start(f32[128]{0:T(128)} %param.9) | copy-start | bytes 1540
